TPU v7x, 256 devices: a whole 4x4x8 slice. The times are simulated.
256 devices in a mesh: pts: 32 (over y, x, core), tm: 8 (over z).
Axes of the slice: x: 4, y: 4, z: 8, core: 2. Of those that a mesh axis runs over, the one named last changes fastest.
Arguments:
- record: float32 [128, 1536, 1024], P('tm', 'pts'), may hold values from -125 to 125
- start_time: float32 [128, 64], replicated, may hold values from -6 to 6
- start_circ: float32 [1024, 128], replicated, may hold values from -6 to 6
Outputs:
- factor_time: float32 [128, 64], replicated
- factor_circ: float32 [1024, 128], replicated
- core_tensor: float32 [64, 1536, 128], P('tm', 'pts')
All inputs are finite; a program needn't handle non-finite values.
Results may differ from a plain program's by a relative error of at most 0.0003.
Values sent between devices are 32-bit elements; how exact they have to be, the bound alone decides.
A program may use at most 64 MiB of HBM per device.

v0:
```python
import jax
import jax.numpy as jnp
from jax import lax
from jax.sharding import PartitionSpec as P

ITERS = 3


def orthonormal_iteration(gram_full, start):
    basis_now = start
    for repeat in range(ITERS):
        grown_full = jnp.dot(gram_full, basis_now, precision=lax.Precision.HIGHEST)
        inner_sum = jnp.dot(grown_full.T, grown_full, precision=lax.Precision.HIGHEST)
        factor_low = jnp.linalg.cholesky(inner_sum)
        basis_now = jax.scipy.linalg.solve_triangular(factor_low, grown_full.T, lower=True).T
    return basis_now


def local(record, start_time, start_circ):
    exchanged = lax.all_to_all(record, "tm", split_axis=2, concat_axis=0, tiled=True)
    time_part = jnp.einsum("tpc,spc->ts", exchanged, exchanged, precision=lax.Precision.HIGHEST)
    gram_time = lax.psum(time_part, ("pts", "tm"))
    factor_time = orthonormal_iteration(gram_time, start_time)
    reduced = jnp.einsum("tr,tpc->rpc", factor_time, exchanged, precision=lax.Precision.HIGHEST)
    reduced_back = lax.all_to_all(reduced, "tm", split_axis=0, concat_axis=2, tiled=True)
    circ_part = jnp.einsum(
        "rpc,rpd->cd", reduced_back, reduced_back, precision=lax.Precision.HIGHEST
    )
    gram_circ = lax.psum(circ_part, ("pts", "tm"))
    factor_circ = orthonormal_iteration(gram_circ, start_circ)
    core_tensor = jnp.einsum(
        "rpc,ck->rpk", reduced_back, factor_circ, precision=lax.Precision.HIGHEST
    )
    return (factor_time, factor_circ, core_tensor)


def solution(mesh):
    placed = (P("tm", "pts", None), P(), P())
    return jax.shard_map(
        local,
        mesh=mesh,
        in_specs=placed,
        out_specs=(P(), P(), P("tm", "pts", None)),
        check_vma=False,
    )
```

profile of v0, /device:TPU:25, one launch (start us, length us, event | category | flops | bytes accessed | tf_op | source)
XLA Modules:
  0.0 841.0 jit_solution(16209880583528596403)
XLA Ops:
  7.2 7.9 copy.15
  15.1 11.3 %reshape.26 = f32[8,1,98304]{2,1,0:T(1,128)} reshape(f32[1024,16,48]{2,1,0:T(8,128)} %bitcast.129) | data formatting | bytes 6291456
  26.4 80.5 %all_to_all.36 = f32[8,1,98304]{2,1,0:T(1,128)} all-to-all(f32[8,1,98304]{2,1,0:T(1,128)} %reshape.26), channel_id=1, replica_groups=mesh['pts'=32,'tm'=8] {'tm'}, dimensions={0} | all-to-all | bytes 6291456 | tf_op jit(solution)/shard_map/all_to_all | solution.py:20
  106.9 0.5 broadcast.72
  107.4 11.8 %reduce.8 = f32[8,98304]{1,0:T(8,128)} reduce(f32[8,1,98304]{2,1,0:T(1,128)} %all_to_all.36, f32[]{:T(128)} %broadcast.72), dimensions={1}, to_apply=%all_to_all.26.reduce_sub_computation | reduce | bytes 6291460 | tf_op jit(solution)/shard_map/all_to_all | solution.py:20
  119.1 8.5 %reshape.27 = f32[1024,16,48]{2,1,0:T(8,128)} reshape(f32[8,98304]{1,0:T(8,128)} %reduce.8) | data formatting | bytes 6291456
  127.6 7.8 copy.16
  135.5 6.3 convolution_bitcast_fusion.1
  141.8 234.8 %all-reduce.3.cloned.1.call-done = f32[128,128]{1,0:T(8,128)} async-done(((f32[128,128]{1,0:T(8,128)}), f32[128,128]{1,0:T(8,128)}) %all-reduce.3.cloned.1.call-update) | async-done | bytes 65552 | tf_op jit(solution)/shard_map/psum | solution.py:22
  376.6 1.1 fusion.42
  377.7 0.2 fusion.43
  377.9 0.1 copy.17
  377.9 5.8 cholesky.116
  383.8 0.6 compare_reduce_fusion.5
  384.5 0.7 fusion.21
  385.1 4.9 custom-call.14
  390.0 0.3 fusion.34
  390.3 1.1 fusion.44
  391.4 0.2 fusion.45
  391.7 5.8 cholesky.127
  397.5 0.6 compare_reduce_fusion.4
  398.2 0.7 fusion.22
  398.8 4.9 custom-call.15
  403.7 0.3 fusion.30
  404.0 1.1 fusion.46
  405.1 0.2 fusion.47
  405.4 5.8 cholesky.138
  411.3 0.6 compare_reduce_fusion.3
  411.9 0.7 fusion.23
  412.6 4.9 custom-call.16
  417.5 0.3 fusion.26
  417.7 3.7 fusion.24
  421.4 0.9 copy.20
  422.3 40.8 %all_to_all.37 = f32[64,48,128]{2,1,0:T(8,128)S(1)} all-to-all(f32[64,48,128]{2,1,0:T(8,128)S(1)} %copy.20), channel_id=1, replica_groups=mesh['pts'=32,'tm'=8] {'tm'}, dimensions={0} | all-to-all | bytes 3145728 | tf_op jit(solution)/shard_map/all_to_all | solution.py:25
  463.2 2.1 copy.27
  465.2 1.5 all_to_all.33
  466.8 8.3 convolution_bitcast_fusion
  475.1 265.3 %all-reduce.5.cloned.1.call-done = f32[1024,1024]{1,0:T(8,128)} async-done(((f32[1024,1024]{1,0:T(8,128)}), f32[1024,1024]{1,0:T(8,128)}) %all-reduce.5.cloned.1.call-update) | async-done | bytes 4194320 | tf_op jit(solution)/shard_map/psum | solution.py:29
  740.4 5.4 fusion.48
  745.8 1.0 fusion.49
  746.8 0.1 copy.22
  746.9 11.7 %cholesky.149 = f32[128,128]{1,0:T(8,128)S(1)} custom-call(f32[128,128]{1,0:T(8,128)S(1)} %fusion.16), custom_call_target="Cholesky" | custom-call | tf_op jit(solution)/shard_map/jit(cholesky)/cholesky | solution.py:14
  758.6 0.6 compare_reduce_fusion.2
  759.3 0.7 fusion.8
  759.9 9.8 %custom-call.17 = f32[1,128,128]{1,2,0:T(8,128)S(1)} custom-call(f32[1,128,128]{2,1,0:T(8,128)S(1)} %fusion.8), custom_call_target="InvertDiagBlocksLowerTriangular" | custom-call | tf_op jit(solution)/shard_map/jit(_solve_triangular)/triangular_solve | solution.py:15
  769.8 0.6 fusion.6
  770.4 5.4 fusion.50
  775.8 1.0 fusion.51
  776.9 0.1 copy.23
  777.0 11.7 %cholesky.160 = f32[128,128]{1,0:T(8,128)S(1)} custom-call(f32[128,128]{1,0:T(8,128)S(1)} %fusion.14), custom_call_target="Cholesky" | custom-call | tf_op jit(solution)/shard_map/jit(cholesky)/cholesky | solution.py:14
  788.7 0.6 compare_reduce_fusion.1
  789.4 0.7 fusion.9
  790.0 9.8 %custom-call.18 = f32[1,128,128]{1,2,0:T(8,128)S(1)} custom-call(f32[1,128,128]{2,1,0:T(8,128)S(1)} %fusion.9), custom_call_target="InvertDiagBlocksLowerTriangular" | custom-call | tf_op jit(solution)/shard_map/jit(_solve_triangular)/triangular_solve | solution.py:15
  799.8 0.6 fusion.4
  800.5 5.5 fusion.52
  806.0 1.0 fusion.53
  807.0 0.1 copy.24
  807.1 11.7 %cholesky.171 = f32[128,128]{1,0:T(8,128)S(1)} custom-call(f32[128,128]{1,0:T(8,128)S(1)} %fusion.12), custom_call_target="Cholesky" | custom-call | tf_op jit(solution)/shard_map/jit(cholesky)/cholesky | solution.py:14
  818.8 0.6 compare_reduce_fusion
  819.5 0.7 fusion.10
  820.2 9.8 %custom-call.19 = f32[1,128,128]{1,2,0:T(8,128)S(1)} custom-call(f32[1,128,128]{2,1,0:T(8,128)S(1)} %fusion.10), custom_call_target="InvertDiagBlocksLowerTriangular" | custom-call | tf_op jit(solution)/shard_map/jit(_solve_triangular)/triangular_solve | solution.py:15
  830.0 0.6 fusion.2
  830.6 2.1 fusion
  832.7 1.0 copy.25
  (24 shorter events, 0.5 us)
Async XLA Ops:
  7.2 733.2 %copy-start = (f32[1024,128]{1,0:T(8,128)S(1)}, f32[1024,128]{1,0:T(8,128)}, u32[]{:S(2)}) copy-start(f32[1024,128]{1,0:T(8,128)} %param.11) | copy-start | bytes 1572868
  7.2 369.4 %all-reduce.3.cloned.1.call-start = ((), (), s32[]{:S(2)}) async-start(), calls=%async_computation.2 | async-start | bytes 131072 | tf_op jit(solution)/shard_map/psum | solution.py:22
  135.4 241.1 %copy-start.2 = (f32[128,64]{0,1:T(8,128)S(1)}, f32[128,64]{0,1:T(8,128)}, u32[]{:S(2)}) copy-start(f32[128,64]{0,1:T(8,128)} %param.10) | copy-start | bytes 98308
  141.8 598.6 %all-reduce.5.cloned.1.call-start = ((), (), s32[]{:S(2)}) async-start(), calls=%async_computation.3 | async-start | bytes 8388608 | tf_op jit(solution)/shard_map/psum | solution.py:29
  417.7 4.6 copy-start.1
Sparse Core Ops, SparseCore 0:
  141.9 234.6 all-reduce.2
  475.2 265.1 all-reduce.4
where the time goes:
time: 853 us; the launch traced here: 841 us
  waiting for transfers between devices  500 us (59%)
  blocking collectives  121 us (14%)
  other arithmetic  117 us (14%)
  matrix products  46.1 us (5%)
  local copies, waits for them, and re-layouts  42 us (5%)
  between operations  14.8 us (2%)
    psum x1, waiting for transfers between devices, local(): gram_circ = lax.psum(circ_part, ('pts', 'tm'))  265 us
    psum x1, waiting for transfers between devices, local(): gram_time = lax.psum(time_part, ('pts', 'tm'))  235 us
    all_to_all x1, blocking collectives, local(): lax.all_to_all(record, 'tm', split_axis=2, concat_axis=0, tiled=True)  80.5 us
    another operation x18, other arithmetic, orthonormal_iteration(): factor_low = jnp.linalg.cholesky(inner_sum)  56.7 us
    another operation x12, other arithmetic, orthonormal_iteration(): jax.scipy.linalg.solve_triangular(factor_low, grown_full.T, lower=True)  48 us
    all_to_all x1, blocking collectives, local(): lax.all_to_all(reduced, 'tm', split_axis=0, concat_axis=2, tiled=True)  40.8 us
    unnamed x10, local copies, waits for them, and re-layouts  28.7 us
    dot_general x6, matrix products, orthonormal_iteration(): grown_full = jnp.dot(gram_full, basis_now, precision=lax.Precision.HIGHEST)  19.5 us
  transfers between devices with their start and end apart: 2, of which 2 were waited for; matrix products, arithmetic and copies ran while one was open for 0% of the time, Pallas kernels for 0%

commit v1 on v0

v1 whole, which is shorter than its diff:
```python
import functools

import jax
import jax.numpy as jnp
from jax import lax
from jax.experimental import pallas as pl
from jax.experimental.pallas import tpu as pltpu
from jax.sharding import PartitionSpec as P

ITERS = 3
MESH = pl.DeviceIdType.MESH
HI = lax.Precision.HIGHEST
F32 = jnp.float32
VM = pltpu.VMEM
LIMIT = 56 * 1024 * 1024
CHUNKS = 2
BLOCKS = 36


def dot(a, b, dims=((1,), (0,))):
    return lax.dot_general(a, b, (dims, ((), ())), precision=HI, preferred_element_type=F32)


def place():
    pts = lax.axis_index("pts")
    return pts // 8, (pts // 2) % 4, pts % 2, lax.axis_index("tm")


def device(y, x, c, z):
    return (y * 8 + x * 2 + c, z)


def greet(peers):
    barrier = pltpu.get_barrier_semaphore()
    for peer in peers:
        pl.semaphore_signal(barrier, inc=1, device_id=peer, device_id_type=MESH)
    pl.semaphore_wait(barrier, len(peers))


def send(src, dst, ssem, rsem, peer):
    copy = pltpu.make_async_remote_copy(
        src_ref=src, dst_ref=dst, send_sem=ssem, recv_sem=rsem, device_id=peer, device_id_type=MESH
    )
    copy.start()
    return copy


def exchange_kernel(rec, ex, gram, stage, part, col, plane, xs, xr, gs, gr):
    y, x, c, z = place()
    m = z * 2 + c
    q = y * 4 + x

    def column(d):
        other = (m + d) % 16
        return other, device(y, x, other % 2, other // 2)

    def flat(d):
        other = (q + d) % 16
        return device(other // 4, other % 4, c, z)

    greet([column(d)[1] for d in range(1, 16)] + [flat(d) for d in range(1, 16)])
    for zz in range(8):
        for p in range(6):
            for h in range(2):
                point = 6 * zz + p
                for b in range(8):
                    first = h * 8 * 384 + point // 8 * 64 + b * 8 + point % 8
                    stage[zz, p, pl.ds(8 * h, 8), 128 * b : 128 * (b + 1)] = rec[pl.ds(first, 8, stride=384), :]
    width = 6 // CHUNKS
    copies = []
    for k in range(CHUNKS):
        some = pl.ds(k * width, width)
        for d in (4, 3, 5, 2, 6, 1, 7):
            to = (z + d) % 8
            copies.append(
                (k, send(stage.at[to, some], ex.at[z, some], xs.at[k, d], xr.at[k, d], device(y, x, c, to)))
            )
    ex[z] = stage[z]
    total = jnp.zeros((128, 128), F32)
    for k in range(CHUNKS):
        for kk, copy in copies:
            if kk == k:
                copy.wait_recv()
        for p in range(k * width, (k + 1) * width):
            slab = ex[:, p].reshape(128, 1024)
            total = total + dot(slab, slab, ((1,), (1,)))
    for _, copy in copies:
        copy.wait_send()
    part[...] = total.reshape(16, 8, 128)
    copies = []
    for d in range(1, 16):
        other, peer = column(d)
        copies.append(send(part.at[other], col.at[m], gs.at[0, d], gr.at[0, d], peer))
    col[m] = part[m]
    for copy in copies:
        copy.wait()
    plane[q] = jnp.sum(col[...], axis=0)
    copies = []
    for d in range(1, 16):
        copies.append(send(plane.at[q], plane.at[q], gs.at[1, d], gr.at[1, d], flat(d)))
    for copy in copies:
        copy.wait()
    gram[m] = jnp.sum(plane[...], axis=0)
    copies = []
    for d in range(1, 16):
        copies.append(send(gram.at[m], gram.at[m], gs.at[2, d], gr.at[2, d], column(d)[1]))
    for copy in copies:
        copy.wait()


def exchange(record):
    return pl.pallas_call(
        exchange_kernel,
        out_shape=(jax.ShapeDtypeStruct((8, 6, 16, 1024), F32), jax.ShapeDtypeStruct((16, 8, 128), F32)),
        in_specs=[pl.BlockSpec(memory_space=VM)],
        out_specs=(pl.BlockSpec(memory_space=VM), pl.BlockSpec(memory_space=VM)),
        scratch_shapes=[
            VM((8, 6, 16, 1024), F32),
            VM((16, 8, 128), F32),
            VM((16, 8, 128), F32),
            VM((16, 8, 128), F32),
            pltpu.SemaphoreType.DMA((CHUNKS, 8)),
            pltpu.SemaphoreType.DMA((CHUNKS, 8)),
            pltpu.SemaphoreType.DMA((3, 16)),
            pltpu.SemaphoreType.DMA((3, 16)),
        ],
        compiler_params=pltpu.CompilerParams(collective_id=0, has_side_effects=True, vmem_limit_bytes=LIMIT),
        name="exchange",
    )(record)


def lower_inverse(w):
    n = w.shape[0]
    rows = lax.broadcasted_iota(jnp.int32, (8, 1), 0)
    eye = (lax.broadcasted_iota(jnp.int32, (n, n), 0) == lax.broadcasted_iota(jnp.int32, (n, n), 1)).astype(F32)
    both = jnp.concatenate([w, eye], axis=1)
    tiles = [both[8 * i : 8 * i + 8] for i in range(n // 8)]
    diag = []
    for j in range(n):
        own, inside = j // 8, j % 8
        row = tiles[own][inside : inside + 1]
        pivot = row[:, j : j + 1]
        diag.append(pivot)
        scaled = row * (1.0 / pivot)
        for i in range(own, n // 8):
            column = tiles[i][:, j : j + 1]
            if i == own:
                column = jnp.where(rows > inside, column, 0.0)
            tiles[i] = tiles[i] - column * scaled
    out = []
    for i in range(n // 8):
        d = jnp.concatenate(diag[8 * i : 8 * i + 8], axis=0)
        out.append(tiles[i][:, n:] * lax.rsqrt(d))
    return jnp.concatenate(out, axis=0)


def time_kernel(ex, gram, start, factor, reduced, circ, turned):
    g = gram[...].reshape(128, 128)
    factor[...] = start[...]

    def step(i, carry):
        grown = dot(g, factor[...])
        inner = dot(grown, grown, ((0,), (0,)))
        factor[...] = dot(grown, lower_inverse(inner), ((1,), (1,)))
        return carry

    lax.fori_loop(0, ITERS, step, 0)
    across = factor[...].T
    for p in range(6):
        reduced[pl.ds(64 * p, 64), :] = dot(across, ex[:, p].reshape(128, 1024))
    turned[...] = reduced[...].T
    for i in range(8):
        wide = dot(turned[pl.ds(128 * i, 128), :], reduced[:, : 128 * (i + 1)])
        for j in range(i + 1):
            circ[i * (i + 1) // 2 + j] = wide[:, 128 * j : 128 * (j + 1)]


def time_part(ex, gram, start):
    return pl.pallas_call(
        time_kernel,
        out_shape=(
            jax.ShapeDtypeStruct((128, 64), F32),
            jax.ShapeDtypeStruct((384, 1024), F32),
            jax.ShapeDtypeStruct((BLOCKS, 128, 128), F32),
        ),
        in_specs=[pl.BlockSpec(memory_space=VM)] * 3,
        out_specs=(pl.BlockSpec(memory_space=VM),) * 3,
        scratch_shapes=[VM((1024, 384), F32)],
        compiler_params=pltpu.CompilerParams(vmem_limit_bytes=LIMIT),
        name="time_part",
    )(ex, gram, start)


Y, X, C, Z = (0, 4), (1, 4), (2, 2), (3, 8)
PARTS = (
    (0, 256, (C, X, Y, Z)),
    (256, 256, (C, Y, X, Z)),
    (512, 64, (C, Z, X, Y)),
)


def sum_kernel(part, out, *scratch):
    here = place()

    def peer(axis, d):
        at = list(here)
        at[axis[0]] = (here[axis[0]] + d) % axis[1]
        return at[axis[0]], device(*at)

    greet([peer(axis, d)[1] for axis in (Y, X, C, Z) for d in range(1, axis[1])])
    places = [base for base, _, _ in PARTS]
    sizes = [size for _, size, _ in PARTS]
    bufs = [scratch[4 * n : 4 * n + 4] for n in range(3)]
    accs = scratch[12:15]
    ss, rs = scratch[15], scratch[16]
    trail = [[], [], []]
    for step in range(4):
        going = []
        for n, (_, _, order) in enumerate(PARTS):
            axis = order[step]
            me = here[axis[0]]
            split = sizes[n] % axis[1] == 0
            piece = sizes[n] // axis[1] if split else sizes[n]
            buf = bufs[n][step]
            src = part if step == 0 else accs[n]
            origin = places[n] if step == 0 else 0
            copies = []
            for d in range(1, axis[1]):
                other, dev = peer(axis, d)
                at = origin + other * piece if split else origin
                copies.append(
                    send(src.at[pl.ds(at, piece)], buf.at[me], ss.at[n, step, d], rs.at[n, step, d], dev)
                )
            mine = origin + me * piece if split else origin
            buf[me] = src[pl.ds(mine, piece)]
            going.append((n, axis, me, split, piece, buf, copies))
        for n, axis, me, split, piece, buf, copies in going:
            for copy in copies:
                copy.wait()
            value = buf[0]
            for k in range(1, axis[1]):
                value = value + buf[k]
            trail[n].append((axis, places[n], sizes[n], split))
            if split:
                places[n] = places[n] + me * piece
                sizes[n] = piece
            if step < 3:
                accs[n][pl.ds(0, piece)] = value
            else:
                out[pl.ds(places[n], piece)] = value
    for step in (3, 2, 1, 0):
        going = []
        for n in range(3):
            axis, was, size, split = trail[n][step]
            if split:
                some = out.at[pl.ds(places[n], sizes[n])]
                for d in range(1, axis[1]):
                    going.append(send(some, some, ss.at[n, 4 + step, d], rs.at[n, 4 + step, d], peer(axis, d)[1]))
                places[n], sizes[n] = was, size
        for copy in going:
            copy.wait()


def sum_parts(part):
    bufs, accs = [], []
    for _, size, order in PARTS:
        for step, axis in enumerate(order):
            if size % axis[1] == 0:
                size = size // axis[1]
            bufs.append(VM((axis[1], size, 8, 128), F32))
            if step == 0:
                accs.append(VM((size, 8, 128), F32))
    return pl.pallas_call(
        sum_kernel,
        out_shape=jax.ShapeDtypeStruct((BLOCKS * 16, 8, 128), F32),
        in_specs=[pl.BlockSpec(memory_space=VM)],
        out_specs=pl.BlockSpec(memory_space=VM),
        scratch_shapes=[
            *bufs,
            *accs,
            pltpu.SemaphoreType.DMA((3, 8, 8)),
            pltpu.SemaphoreType.DMA((3, 8, 8)),
        ],
        compiler_params=pltpu.CompilerParams(collective_id=1, has_side_effects=True, vmem_limit_bytes=LIMIT),
        name="sum_parts",
    )(part)


def circ_kernel(tri, start, reduced, factor, core, full):
    for i in range(8):
        for j in range(i + 1):
            block = tri[i * (i + 1) // 2 + j]
            full[pl.ds(128 * i, 128), 128 * j : 128 * (j + 1)] = block
            if j < i:
                full[pl.ds(128 * j, 128), 128 * i : 128 * (i + 1)] = block.T
    factor[...] = start[...]

    def step(i, carry):
        grown = dot(full[...], factor[...])
        inner = dot(grown, grown, ((0,), (0,)))
        factor[...] = dot(grown, lower_inverse(inner), ((1,), (1,)))
        return carry

    lax.fori_loop(0, ITERS, step, 0)
    for p in range(6):
        here = dot(reduced[pl.ds(64 * p, 64), :], factor[...])
        for k in range(8):
            core[k, p] = here[8 * k : 8 * k + 8]


def circ_part(tri, start, reduced):
    return pl.pallas_call(
        circ_kernel,
        out_shape=(jax.ShapeDtypeStruct((1024, 128), F32), jax.ShapeDtypeStruct((8, 6, 8, 128), F32)),
        in_specs=[pl.BlockSpec(memory_space=VM)] * 3,
        out_specs=(pl.BlockSpec(memory_space=VM),) * 2,
        scratch_shapes=[VM((1024, 1024), F32)],
        compiler_params=pltpu.CompilerParams(vmem_limit_bytes=LIMIT),
        name="circ_part",
    )(tri, start, reduced)


def return_kernel(core, out, got, ss, rs):
    y, x, c, z = place()
    greet([device(y, x, c, (z + d) % 8) for d in range(1, 8)])
    copies = []
    for d in (4, 3, 5, 2, 6, 1, 7):
        to = (z + d) % 8
        copies.append(send(core.at[to], got.at[z], ss.at[d], rs.at[d], device(y, x, c, to)))
    got[z] = core[z]
    for copy in copies:
        copy.wait()
    for k in range(8):
        for p in range(6):
            out[pl.ds(6 * k + p, 8, stride=48), :] = got[k, p]


def return_core(core):
    return pl.pallas_call(
        return_kernel,
        out_shape=jax.ShapeDtypeStruct((384, 128), F32),
        in_specs=[pl.BlockSpec(memory_space=VM)],
        out_specs=pl.BlockSpec(memory_space=VM),
        scratch_shapes=[
            VM((8, 6, 8, 128), F32),
            pltpu.SemaphoreType.DMA((8,)),
            pltpu.SemaphoreType.DMA((8,)),
        ],
        compiler_params=pltpu.CompilerParams(collective_id=2, has_side_effects=True, vmem_limit_bytes=LIMIT),
        name="return_core",
    )(core)


def local(record, start_time, start_circ):
    rows = record.reshape(96, 8, 8, 128).transpose(0, 2, 1, 3).reshape(6144, 128)
    ex, gram = exchange(rows)
    factor_time, reduced, part = time_part(ex, gram, start_time)
    tri = sum_parts(part.reshape(BLOCKS * 16, 8, 128))
    factor_circ, core = circ_part(tri.reshape(BLOCKS, 128, 128), start_circ, reduced)
    core = return_core(core).reshape(8, 48, 128)
    return (factor_time, factor_circ, core)


def solution(mesh):
    placed = (P("tm", "pts", None), P(), P())
    return jax.shard_map(
        local,
        mesh=mesh,
        in_specs=placed,
        out_specs=(P(), P(), P("tm", "pts", None)),
        check_vma=False,
    )
```

time: 853 us -> 253 us (0.30); the launches traced: 841 us -> 251 us
  waiting for transfers between devices: 500 us -> 0 us
  Pallas kernels: 0 us -> 246 us
  blocking collectives: 121 us -> 0 us
  other arithmetic: 117 us -> 0 us
  matrix products: 46.1 us -> 0 us
  local copies, waits for them, and re-layouts: 42 us -> 4.64 us
  between operations: 14.8 us -> 0.66 us
    psum x2 -> x0, waiting for transfers between devices: 500 us -> none  [the longest x1 265 us: local(): gram_circ = lax.psum(circ_part, ('pts', 'tm'))]
    pallas_call x0 -> x5, Pallas kernels: none -> 246 us  [the longest x1 102 us: exchange(): pl.pallas_call(exchange_kernel, out_shape=(jax.ShapeDtypeStruct((8, 6, 16...]
    all_to_all x2 -> x0, blocking collectives: 121 us -> none  [the longest x1 80.5 us: local(): lax.all_to_all(record, 'tm', split_axis=2, concat_axis=0, tiled=True)]
    another operation x30 -> x0, other arithmetic: 105 us -> none  [the longest x18 56.7 us: orthonormal_iteration(): factor_low = jnp.linalg.cholesky(inner_sum)]
    dot_general x16 -> x0, matrix products: 43.4 us -> none  [the longest x6 19.5 us: orthonormal_iteration(): grown_full = jnp.dot(gram_full, basis_now, precision=lax.Precision.HIGHEST)]
    unnamed x10 -> x3, local copies, waits for them, and re-layouts: 28.7 us -> 4.64 us
    all_to_all x4 -> x0, local copies, waits for them, and re-layouts: 11.9 us -> none  [the longest x2 8.33 us: local(): lax.all_to_all(record, 'tm', split_axis=2, concat_axis=0, tiled=True)]
    all_to_all x1 -> x0, other arithmetic: 11.8 us -> none  [local(): lax.all_to_all(record, 'tm', split_axis=2, concat_axis=0, tiled=True)]
  transfers between devices with their start and end apart: 2 -> 0, of which waited for: 2 -> 0; matrix products, arithmetic and copies ran while one was open for 0% -> 0% of each run, Pallas kernels for 0% -> 0%
where the time goes in v1:
time: 253 us; the launch traced here: 251 us
  Pallas kernels  246 us (97%)
  local copies, waits for them, and re-layouts  4.64 us (2%)
    pallas_call x1, Pallas kernels, exchange(): pl.pallas_call(exchange_kernel, out_shape=(jax.ShapeDtypeStruct((8, 6, 16...  102 us
    pallas_call x1, Pallas kernels, circ_part(): pl.pallas_call(circ_kernel, out_shape=(jax.ShapeDtypeStruct((1024, 128),...  55.9 us
    pallas_call x1, Pallas kernels, sum_parts(): pl.pallas_call(sum_kernel, out_shape=jax.ShapeDtypeStruct((BLOCKS * 16, 8...  49.7 us
    pallas_call x1, Pallas kernels, time_part(): pl.pallas_call(time_kernel, out_shape=(jax.ShapeDtypeStruct((128, 64), F3...  28 us
    pallas_call x1, Pallas kernels, return_core(): pl.pallas_call(return_kernel, out_shape=jax.ShapeDtypeStruct((384, 128),...  10.6 us

profile of v1, /device:TPU:25, one launch (start us, length us, event | category | flops | bytes accessed | tf_op | source)
XLA Modules:
  0.0 251.3 jit_solution(850524706482699043)
XLA Ops:
  0.6 1.5 copy.6.start
  2.1 101.7 %exchange.1 = (f32[8,6,16,1024]{3,2,1,0:T(8,128)}, f32[16,8,128]{2,1,0:T(8,128)}) custom-call(f32[6144,128]{1,0:T(8,128)} %bitcast.9), custom_call_target="tpu_custom_call" | custom-call | tf_op jit(solution)/shard_map/exchange/pallas_call | solution.py:112
  103.8 28.0 %time_part.1 = (f32[128,64]{1,0:T(8,128)}, f32[384,1024]{1,0:T(8,128)}, f32[36,128,128]{2,1,0:T(8,128)}) custom-call(f32[8,6,16,1024]{3,2,1,0:T(8,128)} %get-tuple-element.10.ex, f32[16,8,128]{2,1,0:T(8,128)} %get-tuple-element.11.gram, f32[128,64]{1,0:T(8,128)} %copy.6.start), custom_call_target="tpu_custom_call" | custom-call | tf_op jit(solution)/shard_map/time_part/pallas_call | solution.py:179
  131.8 1.5 copy.7
  133.4 49.7 %sum_parts.1 = f32[576,8,128]{2,1,0:T(8,128)} custom-call(f32[576,8,128]{2,1,0:T(8,128)} %bitcast.10), custom_call_target="tpu_custom_call" | custom-call | tf_op jit(solution)/shard_map/sum_parts/pallas_call | solution.py:273
  183.1 55.9 %circ_part.1 = (f32[1024,128]{1,0:T(8,128)}, f32[8,6,8,128]{3,2,1,0:T(8,128)}) custom-call(f32[36,128,128]{2,1,0:T(8,128)} %bitcast.8, f32[1024,128]{1,0:T(8,128)} %start.2, f32[384,1024]{1,0:T(8,128)} %get-tuple-element.14.reduced), custom_call_target="tpu_custom_call" | custom-call | tf_op jit(solution)/shard_map/circ_part/pallas_call | solution.py:312
  239.0 10.6 %return_core.1 = f32[384,128]{1,0:T(8,128)} custom-call(f32[8,6,8,128]{3,2,1,0:T(8,128)} %get-tuple-element.16.core), custom_call_target="tpu_custom_call" | custom-call | tf_op jit(solution)/shard_map/return_core/pallas_call | solution.py:339
  249.6 1.6 copy.9

commit v2 on v0

v2 whole, which is shorter than its diff:
```python
import functools

import jax
import jax.numpy as jnp
from jax import lax
from jax.experimental import pallas as pl
from jax.experimental.pallas import tpu as pltpu
from jax.sharding import PartitionSpec as P

ITERS = 3
MESH = pl.DeviceIdType.MESH
HI = lax.Precision.HIGHEST
F32 = jnp.float32
BF16 = jnp.bfloat16
VM = pltpu.VMEM
LIMIT = 56 * 1024 * 1024
CHUNKS = 6
WIDTH = 6 // CHUNKS
TERMS = ((0, 0), (0, 1), (1, 0), (0, 2), (1, 1), (2, 0))
BLOCKS = 36


def dot(a, b, dims=((1,), (0,))):
    return lax.dot_general(a, b, (dims, ((), ())), precision=HI, preferred_element_type=F32)


def place():
    pts = lax.axis_index("pts")
    return pts // 8, (pts // 2) % 4, pts % 2, lax.axis_index("tm")


def device(y, x, c, z):
    return (y * 8 + x * 2 + c, z)


def send(src, dst, ssem, rsem, peer):
    copy = pltpu.make_async_remote_copy(
        src_ref=src, dst_ref=dst, send_sem=ssem, recv_sem=rsem, device_id=peer, device_id_type=MESH
    )
    copy.start()
    return copy


def lower_inverse(w):
    n = w.shape[0]
    count = n // 8
    lane = lax.broadcasted_iota(jnp.int32, (8, 128), 1)
    sub = lax.broadcasted_iota(jnp.int32, (8, 128), 0)

    def unit(i):
        return (lane == sub + 8 * i + 128 - n).astype(F32)

    if n == 128:
        parts = [[w[8 * i : 8 * i + 8] for i in range(count)], [unit(i) for i in range(count)]]
    else:
        both = jnp.concatenate([w, jnp.zeros_like(w)], axis=1)
        parts = [[both[8 * i : 8 * i + 8] + unit(i) for i in range(count)]]

    def over_lanes(v, j):
        return jnp.broadcast_to(v[:, j : j + 1], (8, 128))

    def over_rows(v, m):
        return jnp.broadcast_to(v[m : m + 1, :], (8, 128))

    out = []
    for k in range(count):
        columns = [[over_lanes(parts[0][i], 8 * k + l) for l in range(8)] for i in range(k, count)]
        e = [[over_rows(columns[0][l], m) for l in range(m + 1)] for m in range(8)]
        t = [[None] * 8 for _ in range(8)]
        inverse = []
        for l in range(8):
            inverse.append(1.0 / e[l][l])
            for m in range(l + 1, 8):
                f = e[m][l] * inverse[l]
                for j in range(l + 1, m + 1):
                    e[m][j] = e[m][j] - f * e[j][l]
                for j in range(l):
                    t[m][j] = t[m][j] - f * t[l][j]
                t[m][l] = -f
        for part in parts:
            rows = [over_rows(part[k], m) for m in range(8)]
            done = []
            for m in range(8):
                v = rows[m]
                for j in range(m):
                    v = v + t[m][j] * rows[j]
                done.append(v)
            if k < count - 1:
                scaled = [done[m] * inverse[m] for m in range(8)]
                taken = []
                for l in range(8):
                    v = scaled[l]
                    for m in range(l + 1, 8):
                        v = v + t[m][l] * scaled[m]
                    taken.append(v)
                for i in range(k + 1, count):
                    v = part[i]
                    for l in range(8):
                        v = v - columns[i - k][l] * taken[l]
                    part[i] = v
        tile = done[0] * lax.rsqrt(e[0][0])
        for m in range(1, 8):
            tile = jnp.where(sub == m, done[m] * lax.rsqrt(e[m][m]), tile)
        out.append(tile[:, 128 - n :])
    return jnp.concatenate(out, axis=0)


def split(v):
    high = v.astype(BF16)
    rest = v - high.astype(F32)
    middle = rest.astype(BF16)
    return high, middle, (rest - middle.astype(F32)).astype(BF16)


def narrow(a, b):
    return lax.dot_general(a, b, (((1,), (0,)), ((), ())), preferred_element_type=F32)


def iterate(basis, grow):
    def step(i, carry):
        grown = grow(basis[...])
        inner = dot(grown, grown, ((1,), (1,)))
        basis[...] = dot(lower_inverse(inner), grown)
        return carry

    lax.fori_loop(0, ITERS, step, 0)


Y, X, C, Z = (0, 4), (1, 4), (2, 2), (3, 8)
PARTS = (
    (0, 256, (C, X, Y, Z)),
    (256, 256, (C, Y, X, Z)),
    (512, 64, (C, Z, X, Y)),
)


def first_kernel(
    rec, start, start_circ, basis, factor, mine, stage, ex, part, col, plane, gram, reduced, left, right, circ, tri, *scratch
):
    one, two, three, xs, xr, gs, gr, ms, mr, ss, rs, *scratch = scratch
    here = place()
    y, x, c, z = here
    m = z * 2 + c
    q = y * 4 + x

    def column(d):
        other = (m + d) % 16
        return other, device(y, x, other % 2, other // 2)

    def flat(d):
        other = (q + d) % 16
        return device(other // 4, other % 4, c, z)

    barrier = pltpu.get_barrier_semaphore()
    for d in range(1, 16):
        pl.semaphore_signal(barrier, inc=1, device_id=column(d)[1], device_id_type=MESH)
        pl.semaphore_signal(barrier, inc=1, device_id=flat(d), device_id_type=MESH)

    for k in range(CHUNKS):
        for zz in range(8):
            for p in range(k * WIDTH, (k + 1) * WIDTH):
                point = 6 * zz + p
                for h in range(2):
                    for b in range(8):
                        at = h * 8 * 384 + point // 8 * 64 + b * 8 + point % 8
                        stage[zz, p, pl.ds(8 * h, 8), 128 * b : 128 * (b + 1)] = rec[pl.ds(at, 8, stride=384), :]
    pl.semaphore_wait(barrier, 30)
    copies = []
    for k in range(CHUNKS):
        some = pl.ds(k * WIDTH, WIDTH)
        for d in (4, 3, 5, 2, 6, 1, 7):
            to = (z + d) % 8
            copies.append(
                (k, send(stage.at[to, some], ex.at[z, some], xs.at[k, d], xr.at[k, d], device(y, x, c, to)))
            )
    ex[z] = stage[z]
    total = jnp.zeros((128, 128), F32)
    for k in range(CHUNKS):
        for kk, copy in copies:
            if kk == k:
                copy.wait_recv()
        for p in range(k * WIDTH, (k + 1) * WIDTH):
            slab = ex[:, p].reshape(128, 1024)
            total = total + dot(slab, slab, ((1,), (1,)))
    started = [copy for _, copy in copies]

    part[...] = total.reshape(16, 8, 128)
    copies = []
    for d in range(1, 16):
        other, peer = column(d)
        copies.append(send(part.at[other], col.at[m], gs.at[0, d], gr.at[0, d], peer))
    col[m] = part[m]
    started += copies
    for copy in copies:
        copy.wait_recv()
    plane[q] = jnp.sum(col[...], axis=0)
    copies = []
    for d in range(1, 16):
        copies.append(send(plane.at[q], plane.at[q], gs.at[1, d], gr.at[1, d], flat(d)))
    started += copies
    for copy in copies:
        copy.wait_recv()
    gram[m] = jnp.sum(plane[...], axis=0)
    copies = []
    for d in range(1, 16):
        copies.append(send(gram.at[m], gram.at[m], gs.at[2, d], gr.at[2, d], column(d)[1]))
    started += copies
    for copy in copies:
        copy.wait_recv()
    for copy in started:
        copy.wait_send()

    g = gram[...].reshape(128, 128)
    factor[...] = start[...]
    iterate(factor, lambda basis: dot(basis, g))
    high, middle, lower = split(factor[...])
    most = jnp.concatenate([high, middle], axis=0)
    whole = jnp.concatenate([high, middle, lower], axis=0)
    for p in range(6):
        first, second, third = split(ex[:, p].reshape(128, 1024))
        u = narrow(whole, first)
        v = narrow(most, second)
        w = narrow(high, third)
        value = u[:64] + ((u[64:128] + v[:64]) + (u[128:] + v[64:] + w))
        reduced[p] = value.reshape(8, 8, 1024)
        pieces = split(value)
        turned = split(value.T)
        for k, (i, j) in enumerate(TERMS):
            left[:, 384 * k + 64 * p : 384 * k + 64 * (p + 1)] = turned[i]
            right[pl.ds(384 * k + 64 * p, 64), :] = pieces[j]
    mine[z] = reduced[:, z]
    returned = []

    def background():
        for d in (4, 3, 5, 2, 6, 1, 7):
            to = (z + d) % 8
            returned.append(send(reduced.at[:, to], mine.at[z], ms.at[d], mr.at[d], device(y, x, c, to)))

    for j in range(4):
        wide = narrow(left[pl.ds(256 * j, 1024 - 256 * j), :], right[:, 256 * j : 256 * (j + 1)])
        for b in (2 * j, 2 * j + 1):
            for a in range(b, 8):
                block = wide[128 * (a - 2 * j) : 128 * (a - 2 * j + 1), 128 * (b - 2 * j) : 128 * (b - 2 * j + 1)]
                circ[pl.ds((a * (a + 1) // 2 + b) * 16, 16)] = block.reshape(16, 8, 128)
    sum_over_devices(here, circ, tri, ss, rs, scratch, background)

    for i in range(8):
        for j in range(i + 1):
            block = tri[pl.ds((i * (i + 1) // 2 + j) * 16, 16)].reshape(128, 128)
            for full, piece in zip((one, two, three), split(block)):
                full[pl.ds(128 * i, 128), 128 * j : 128 * (j + 1)] = piece
            if j < i:
                for full, piece in zip((one, two, three), split(block.T)):
                    full[pl.ds(128 * j, 128), 128 * i : 128 * (i + 1)] = piece
    basis[...] = start_circ[...].T

    def grow(now):
        high, middle, low = split(now)
        a = narrow(jnp.concatenate([high, middle, low], axis=0), one[...])
        b = narrow(jnp.concatenate([high, middle], axis=0), two[...])
        c = narrow(high, three[...])
        return a[:128] + ((a[128:256] + b[:128]) + (a[256:] + b[128:] + c))

    iterate(basis, grow)
    for copy in returned:
        copy.wait()


def sum_over_devices(here, part, out, ss, rs, scratch, background):
    def peer(axis, d):
        at = list(here)
        at[axis[0]] = (here[axis[0]] + d) % axis[1]
        return at[axis[0]], device(*at)

    number = len(PARTS)
    bufs = [scratch[4 * n : 4 * n + 4] for n in range(number)]
    accs = scratch[4 * number : 5 * number]
    started = []
    going = [None] * number
    trail = [[] for _ in PARTS]
    places = [base for base, _, _ in PARTS]
    sizes = [size for _, size, _ in PARTS]

    for n, (base, size, order) in enumerate(PARTS):
        axis, nearby = order[:2]
        piece = size // 2 // nearby[1]
        other, dev = peer(axis, 1)
        going[n] = {}
        for d in (2, 1, 3, 0) if nearby[1] == 4 else (4, 3, 5, 2, 6, 1, 7, 0):
            to = peer(nearby, d)[0]
            some = part.at[pl.ds(base + other * (size // 2) + to * piece, piece)]
            going[n][d] = send(some, bufs[n][0].at[pl.ds(to * piece, piece)], ss.at[n, 0, d], rs.at[n, 0, d], dev)
        started += going[n].values()
    for n, (base, size, order) in enumerate(PARTS):
        axis, nearby = order[:2]
        trail[n].append((axis, base, size, False))
        sizes[n] = size // 2
        places[n] = base + here[axis[0]] * sizes[n]
        trail[n].append((nearby, places[n], sizes[n], False))
        piece = sizes[n] // nearby[1]
        copies = []
        for d, copy in going[n].items():
            copy.wait_recv()
            to, dev = peer(nearby, d)
            some = pl.ds(to * piece, piece)
            accs[n][some] = part[pl.ds(places[n] + to * piece, piece)] + bufs[n][0][some]
            if d:
                copies.append(send(accs[n].at[some], bufs[n][1].at[d], ss.at[n, 1, d], rs.at[n, 1, d], dev))
        going[n] = copies

    def scatter(n, step):
        axis = PARTS[n][2][step]
        me = here[axis[0]]
        buf = bufs[n][step]
        whole = sizes[n] % axis[1] != 0
        piece = sizes[n] if whole else sizes[n] // axis[1]
        copies = []
        for d in range(1, axis[1]):
            other, dev = peer(axis, d)
            some = accs[n].at[pl.ds(0 if whole else other * piece, piece)]
            copies.append(send(some, buf.at[me if whole else d], ss.at[n, step, d], rs.at[n, step, d], dev))
        if whole:
            buf[me] = accs[n][pl.ds(0, piece)]
        going[n] = copies
        trail[n].append((axis, places[n], sizes[n], whole))

    def add(n, step):
        axis, was, size, whole = trail[n][step]
        me = here[axis[0]]
        buf = bufs[n][step]
        for copy in going[n]:
            copy.wait()
        if whole:
            piece = size
            value = buf[0]
        else:
            piece = size // axis[1]
            value = accs[n][pl.ds(me * piece, piece)]
            places[n] = was + me * piece
            sizes[n] = piece
        for k in range(1, axis[1]):
            value = value + buf[k]
        if step == 3:
            out[pl.ds(places[n], piece)] = value
        else:
            accs[n][pl.ds(0, piece)] = value

    def gather(n, step):
        axis, was, size, whole = trail[n][step]
        copies = []
        if not whole:
            some = out.at[pl.ds(places[n], sizes[n])]
            for d in range(1, axis[1]):
                copies.append(send(some, some, ss.at[n, 4 + step, d], rs.at[n, 4 + step, d], peer(axis, d)[1]))
        going[n] = copies
        started.extend(copies)

    def forward(n, d):
        axis = PARTS[n][2][1]
        some = out.at[pl.ds(trail[n][1][1] + peer(axis, axis[1] - d)[0] * sizes[n], sizes[n])]
        return send(some, some, ss.at[n, 4, d], rs.at[n, 4, d], peer(C, 1)[1])

    for step in (1, 2, 3):
        for n in range(number):
            add(n, step)
            if step < 3:
                scatter(n, step + 1)
            else:
                gather(n, 3)
    for step in (2, 1):
        for n in range(number):
            for copy in going[n]:
                copy.wait_recv()
            if not trail[n][step + 1][3]:
                places[n], sizes[n] = trail[n][step + 1][1:3]
            gather(n, step)
            if step == 1:
                going[n] = list(enumerate(going[n], 1)), [forward(n, 0)]
    for n in range(number):
        coming, passed = going[n]
        for d, copy in coming:
            copy.wait_recv()
            passed.append(forward(n, d))
        started += passed
    background()
    for n in range(number):
        for copy in going[n][1]:
            copy.wait_recv()
    for copy in started:
        copy.wait_send()


def first_part(rows, start, start_circ):
    bufs, accs = [], []
    for _, size, order in PARTS:
        for step, axis in enumerate(order):
            if size % axis[1] == 0:
                size = size // axis[1]
            bufs.append(VM((axis[1], size, 8, 128) if step else (size, 8, 128), F32))
            if step == 0:
                accs.append(VM((size, 8, 128), F32))
    dma = pltpu.SemaphoreType.DMA
    return pl.pallas_call(
        first_kernel,
        out_shape=(
            jax.ShapeDtypeStruct((128, 1024), F32),
            jax.ShapeDtypeStruct((64, 128), F32),
            jax.ShapeDtypeStruct((8, 6, 8, 1024), F32),
        ),
        in_specs=[pl.BlockSpec(memory_space=VM)] * 3,
        out_specs=(pl.BlockSpec(memory_space=VM),) * 3,
        scratch_shapes=[
            VM((8, 6, 16, 1024), F32),
            VM((8, 6, 16, 1024), F32),
            VM((16, 8, 128), F32),
            VM((16, 8, 128), F32),
            VM((16, 8, 128), F32),
            VM((16, 8, 128), F32),
            VM((6, 8, 8, 1024), F32),
            VM((1024, 384 * len(TERMS)), BF16),
            VM((384 * len(TERMS), 1024), BF16),
            VM((BLOCKS * 16, 8, 128), F32),
            VM((BLOCKS * 16, 8, 128), F32),
            VM((1024, 1024), BF16),
            VM((1024, 1024), BF16),
            VM((1024, 1024), BF16),
            dma((CHUNKS, 8)),
            dma((CHUNKS, 8)),
            dma((3, 16)),
            dma((3, 16)),
            dma((8,)),
            dma((8,)),
            dma((len(PARTS), 8, 8)),
            dma((len(PARTS), 8, 8)),
            *bufs,
            *accs,
        ],
        compiler_params=pltpu.CompilerParams(collective_id=0, has_side_effects=True, vmem_limit_bytes=LIMIT),
        name="first_part",
    )(rows, start, start_circ)


def core_kernel(basis, mine, early, factor, core, late):
    late[...] = early[...]
    last = basis[...].T
    factor[...] = last
    here = dot(mine[...].reshape(384, 1024), last)
    for k in range(48):
        core[pl.ds(k, 8, stride=48), :] = here[8 * k : 8 * k + 8]


def core_part(basis, mine, early):
    return pl.pallas_call(
        core_kernel,
        out_shape=(
            jax.ShapeDtypeStruct((1024, 128), F32),
            jax.ShapeDtypeStruct((384, 128), F32),
            jax.ShapeDtypeStruct((64, 128), F32),
        ),
        in_specs=[pl.BlockSpec(memory_space=VM)] * 3,
        out_specs=(pl.BlockSpec(memory_space=VM),) * 3,
        compiler_params=pltpu.CompilerParams(vmem_limit_bytes=LIMIT),
        name="core_part",
    )(basis, mine, early)


def local(record, start_time, start_circ):
    rows = record.reshape(96, 8, 8, 128).transpose(0, 2, 1, 3).reshape(6144, 128)
    basis, early, mine = first_part(rows, start_time.T, start_circ)
    factor_circ, core, late = core_part(basis, mine, early)
    return (late.T, factor_circ, core.reshape(8, 48, 128))


def solution(mesh):
    placed = (P("tm", "pts", None), P(), P())
    return jax.shard_map(
        local,
        mesh=mesh,
        in_specs=placed,
        out_specs=(P(), P(), P("tm", "pts", None)),
        check_vma=False,
    )
```

time: 853 us -> 191 us (0.22); the launches traced: 841 us -> 191 us
  waiting for transfers between devices: 500 us -> 0 us
  Pallas kernels: 0 us -> 190 us
  blocking collectives: 121 us -> 0 us
  other arithmetic: 117 us -> 0 us
  matrix products: 46.1 us -> 0 us
  local copies, waits for them, and re-layouts: 42 us -> 0 us
  between operations: 14.8 us -> 0.64 us
    psum x2 -> x0, waiting for transfers between devices: 500 us -> none  [the longest x1 265 us: local(): gram_circ = lax.psum(circ_part, ('pts', 'tm'))]
    pallas_call x0 -> x2, Pallas kernels: none -> 190 us  [the longest x1 187 us: first_part(): pl.pallas_call(first_kernel, out_shape=(jax.ShapeDtypeStruct((128, 1024),...]
    all_to_all x2 -> x0, blocking collectives: 121 us -> none  [the longest x1 80.5 us: local(): lax.all_to_all(record, 'tm', split_axis=2, concat_axis=0, tiled=True)]
    another operation x30 -> x0, other arithmetic: 105 us -> none  [the longest x18 56.7 us: orthonormal_iteration(): factor_low = jnp.linalg.cholesky(inner_sum)]
    dot_general x16 -> x0, matrix products: 43.4 us -> none  [the longest x6 19.5 us: orthonormal_iteration(): grown_full = jnp.dot(gram_full, basis_now, precision=lax.Precision.HIGHEST)]
    unnamed x10 -> x0, local copies, waits for them, and re-layouts: 28.7 us -> none
    all_to_all x4 -> x0, local copies, waits for them, and re-layouts: 11.9 us -> none  [the longest x2 8.33 us: local(): lax.all_to_all(record, 'tm', split_axis=2, concat_axis=0, tiled=True)]
    all_to_all x1 -> x0, other arithmetic: 11.8 us -> none  [local(): lax.all_to_all(record, 'tm', split_axis=2, concat_axis=0, tiled=True)]
  transfers between devices with their start and end apart: 2 -> 0, of which waited for: 2 -> 0; matrix products, arithmetic and copies ran while one was open for 0% -> 0% of each run, Pallas kernels for 0% -> 0%
where the time goes in v2:
time: 191 us
  Pallas kernels  190 us (99%)
    pallas_call x1, Pallas kernels, first_part(): pl.pallas_call(first_kernel, out_shape=(jax.ShapeDtypeStruct((128, 1024),...  187 us

profile of v2, /device:TPU:25, one launch (start us, length us, event | category | flops | bytes accessed | tf_op | source)
XLA Modules:
  0.0 190.9 jit_solution(13828531765917592900)
XLA Ops:
  0.6 186.5 %first_part.1 = (f32[128,1024]{1,0:T(8,128)}, f32[64,128]{1,0:T(8,128)}, f32[8,6,8,1024]{3,2,1,0:T(8,128)}) custom-call(f32[6144,128]{1,0:T(8,128)} %bitcast.8, f32[64,128]{1,0:T(8,128)} %bitcast.9, f32[1024,128]{1,0:T(8,128)} %start_circ.1), custom_call_target="tpu_custom_call" | custom-call | tf_op jit(solution)/shard_map/first_part/pallas_call | solution.py:403
  187.2 3.7 %core_part.1 = (f32[1024,128]{1,0:T(8,128)}, f32[384,128]{1,0:T(8,128)}, f32[64,128]{1,0:T(8,128)}) custom-call(f32[128,1024]{1,0:T(8,128)} %get-tuple-element.9.basis, f32[8,6,8,1024]{3,2,1,0:T(8,128)} %get-tuple-element.10.mine, f32[64,128]{1,0:T(8,128)} %get-tuple-element.11.early), custom_call_target="tpu_custom_call" | custom-call | tf_op jit(solution)/shard_map/core_part/pallas_call | solution.py:453

commit v3 on v2

--- a/solution.py
+++ b/solution.py
@@ -16,7 +16,7 @@
 LIMIT = 56 * 1024 * 1024
 CHUNKS = 6
 WIDTH = 6 // CHUNKS
-TERMS = ((0, 0), (0, 1), (1, 0), (0, 2), (1, 1), (2, 0))
+TERMS = ((0, 0), (0, 1), (1, 0))
 BLOCKS = 36
 
 
@@ -216,6 +216,15 @@
     high, middle, lower = split(factor[...])
     most = jnp.concatenate([high, middle], axis=0)
     whole = jnp.concatenate([high, middle, lower], axis=0)
+    returned = []
+
+    def give_back(k, some):
+        for d in (4, 3, 5, 2, 6, 1, 7):
+            to = (z + d) % 8
+            returned.append(
+                send(reduced.at[some, to], mine.at[z, some], ms.at[k, d], mr.at[k, d], device(y, x, c, to))
+            )
+
     for p in range(6):
         first, second, third = split(ex[:, p].reshape(128, 1024))
         u = narrow(whole, first)
@@ -223,26 +232,21 @@
         w = narrow(high, third)
         value = u[:64] + ((u[64:128] + v[:64]) + (u[128:] + v[64:] + w))
         reduced[p] = value.reshape(8, 8, 1024)
+        if p == 0:
+            give_back(0, pl.ds(0, 1))
         pieces = split(value)
         turned = split(value.T)
         for k, (i, j) in enumerate(TERMS):
             left[:, 384 * k + 64 * p : 384 * k + 64 * (p + 1)] = turned[i]
             right[pl.ds(384 * k + 64 * p, 64), :] = pieces[j]
     mine[z] = reduced[:, z]
-    returned = []
-
-    def background():
-        for d in (4, 3, 5, 2, 6, 1, 7):
-            to = (z + d) % 8
-            returned.append(send(reduced.at[:, to], mine.at[z], ms.at[d], mr.at[d], device(y, x, c, to)))
-
     for j in range(4):
         wide = narrow(left[pl.ds(256 * j, 1024 - 256 * j), :], right[:, 256 * j : 256 * (j + 1)])
         for b in (2 * j, 2 * j + 1):
             for a in range(b, 8):
                 block = wide[128 * (a - 2 * j) : 128 * (a - 2 * j + 1), 128 * (b - 2 * j) : 128 * (b - 2 * j + 1)]
                 circ[pl.ds((a * (a + 1) // 2 + b) * 16, 16)] = block.reshape(16, 8, 128)
-    sum_over_devices(here, circ, tri, ss, rs, scratch, background)
+    sum_over_devices(here, circ, tri, ss, rs, scratch, lambda: give_back(1, pl.ds(1, 5)))
 
     for i in range(8):
         for j in range(i + 1):
@@ -428,8 +432,8 @@
             dma((CHUNKS, 8)),
             dma((3, 16)),
             dma((3, 16)),
-            dma((8,)),
-            dma((8,)),
+            dma((2, 8)),
+            dma((2, 8)),
             dma((len(PARTS), 8, 8)),
             dma((len(PARTS), 8, 8)),
             *bufs,

time: 191 us -> 189 us (0.990)
  no operation moved by 1% of the time
where the time goes in v3:
time: 189 us
  Pallas kernels  189 us (100%)
    pallas_call x1, Pallas kernels, first_part(): pl.pallas_call(first_kernel, out_shape=(jax.ShapeDtypeStruct((128, 1024),...  185 us

profile of v3, /device:TPU:25, one launch (start us, length us, event | category | flops | bytes accessed | tf_op | source)
XLA Modules:
  0.0 189.2 jit_solution(17857304412188146517)
XLA Ops:
  0.6 184.8 %first_part.1 = (f32[128,1024]{1,0:T(8,128)}, f32[64,128]{1,0:T(8,128)}, f32[8,6,8,1024]{3,2,1,0:T(8,128)}) custom-call(f32[6144,128]{1,0:T(8,128)} %bitcast.8, f32[64,128]{1,0:T(8,128)} %bitcast.9, f32[1024,128]{1,0:T(8,128)} %start_circ.1), custom_call_target="tpu_custom_call" | custom-call | tf_op jit(solution)/shard_map/first_part/pallas_call | solution.py:407
  185.4 3.7 %core_part.1 = (f32[1024,128]{1,0:T(8,128)}, f32[384,128]{1,0:T(8,128)}, f32[64,128]{1,0:T(8,128)}) custom-call(f32[128,1024]{1,0:T(8,128)} %get-tuple-element.9.basis, f32[8,6,8,1024]{3,2,1,0:T(8,128)} %get-tuple-element.10.mine, f32[64,128]{1,0:T(8,128)} %get-tuple-element.11.early), custom_call_target="tpu_custom_call" | custom-call | tf_op jit(solution)/shard_map/core_part/pallas_call | solution.py:457
